TPU v7x, 32 devices: a whole 2x2x4 slice. The times are simulated.
32 devices in a mesh: dp: 8 (over z, y), tensor: 4 (over x, core).
Axes of the slice: x: 2, y: 2, z: 4, core: 2. Of those that a mesh axis runs over, the one named last changes fastest.
Arguments:
- inputs: bfloat16 [25600, 768], P(('dp', 'tensor')), may hold values from -6 to 6
- res_ids: int32 [32], P(('dp', 'tensor')), may hold values from 0 to 1
- memory: bfloat16 [2, 6400, 768], P(None, ('dp', 'tensor')), may hold values from -6 to 6
- gain_one: float32 [768], replicated, may hold values from 0.5 to 1.5
- bias_one: float32 [768], replicated, may hold values from -1.8 to 1.8
- w_qkv: bfloat16 [768, 2304], replicated, may hold values from -0.21875 to 0.21875
- b_qkv: float32 [2304], replicated, may hold values from -1.8 to 1.8
- pool_weight: float32 [3, 27, 96], replicated, may hold values from -1.25 to 1.25
- pool_gain: float32 [3, 96], replicated, may hold values from 0.5 to 1.5
- pool_bias: float32 [3, 96], replicated, may hold values from -1.8 to 1.8
- rel_table: float32 [53, 96], replicated, may hold values from -0.6 to 0.6
- w_proj: bfloat16 [768, 768], replicated, may hold values from -0.21875 to 0.21875
- b_proj: float32 [768], replicated, may hold values from -1.8 to 1.8
- gain_two: float32 [768], replicated, may hold values from 0.5 to 1.5
- bias_two: float32 [768], replicated, may hold values from -1.8 to 1.8
- w_up: bfloat16 [768, 3072], P(None, 'tensor'), may hold values from -0.21875 to 0.21875
- b_up: bfloat16 [3072], P('tensor'), may hold values from -1.796875 to 1.796875
- w_down: bfloat16 [3072, 768], P('tensor'), may hold values from -0.109375 to 0.109375
- b_down: float32 [768], replicated, may hold values from -1.8 to 1.8
- cotangent: bfloat16 [25600, 768], P(('dp', 'tensor')), may hold values from -6 to 6
Outputs:
- output: bfloat16 [25600, 768], P(('dp', 'tensor'))
- input_grad: float32 [25600, 768], P(('dp', 'tensor'))
- grad_gain_one: float32 [768], replicated
- grad_bias_one: float32 [768], replicated
- grad_w_qkv: float32 [768, 2304], replicated
- grad_b_qkv: float32 [2304], replicated
- grad_pool_weight: float32 [3, 27, 96], replicated
- grad_pool_gain: float32 [3, 96], replicated
- grad_pool_bias: float32 [3, 96], replicated
- grad_rel_table: float32 [53, 96], replicated
- grad_w_proj: float32 [768, 768], replicated
- grad_b_proj: float32 [768], replicated
- grad_gain_two: float32 [768], replicated
- grad_bias_two: float32 [768], replicated
- grad_w_up: float32 [768, 3072], P(None, 'tensor')
- grad_b_up: float32 [3072], P('tensor')
- grad_w_down: float32 [3072, 768], P('tensor')
- grad_b_down: float32 [768], replicated
Inputs may be any that keep to these rules, and one draw needn't show every extreme that they name: `res_ids`: 0 marks a clip whose frames hold 7 x 7 tokens in the corner of the 10 x 10 grid, 1 a clip that fills it.
All inputs are finite; a program needn't handle non-finite values.
Results may differ from a plain program's by a relative error of at most 0.012.
Values may be sent and summed in bfloat16 or wider, within the bound.
A program may use at most 384 MiB of HBM per device.

v0:
```python
import jax
import jax.numpy as jnp
from jax import lax
from jax.sharding import PartitionSpec as P

D = 768
HEADS = 8
HEAD_DIM = 96
FRAMES = 8
SIDE = 10
SMALL_SIDE = 7
LENGTH = 800
MEM = 200
OFFSETS = 28
REL_ROWS = 53
HIGHEST = lax.Precision.HIGHEST
NORM_EPS = 1e-06
INV_ROOT_TWO = 0.7071067811865476


def layer_norm(values, gain_vec, shift_vec):
    average = jnp.mean(values, axis=-1, keepdims=True)
    centered = values - average
    variance = jnp.mean(centered * centered, axis=-1, keepdims=True)
    return centered * lax.rsqrt(variance + NORM_EPS) * gain_vec + shift_vec


def gelu_exact(values):
    return 0.5 * values * (1.0 + lax.erf(values * INV_ROOT_TWO))


def grid_tables(res_ids):
    position = jnp.arange(LENGTH, dtype=jnp.int32)
    frame_of = position // (SIDE * SIDE)
    row_of = position // SIDE % SIDE
    column_of = position % SIDE
    large_clip = res_ids[:, None] == 1
    inside = (row_of < SMALL_SIDE) & (column_of < SMALL_SIDE)
    token_valid = large_clip | inside[None, :]
    memory_side = (SIDE + 1) // 2
    memory_small = (SMALL_SIDE + 1) // 2
    memory_index = jnp.arange(MEM, dtype=jnp.int32) % (MEM // 2)
    memory_row = memory_index // memory_side % memory_side
    memory_column = memory_index % memory_side
    memory_inside = (memory_row < memory_small) & (memory_column < memory_small)
    memory_valid = large_clip | memory_inside[None, :]
    frame_range = jnp.arange(FRAMES, dtype=jnp.int32)
    side_range = jnp.arange(SIDE, dtype=jnp.int32)
    row_base = 2 * FRAMES - 1
    column_base = row_base + 2 * SIDE - 1
    target = jnp.concatenate(
        [
            frame_of[:, None] - frame_range[None, :] + FRAMES - 1,
            row_base + row_of[:, None] - side_range[None, :] + SIDE - 1,
            column_base + column_of[:, None] - side_range[None, :] + SIDE - 1,
        ],
        axis=1,
    )
    select_table = (
        target[:, :, None] == jnp.arange(REL_ROWS, dtype=jnp.int32)[None, None, :]
    ).astype(jnp.float32)
    key_onehot = jnp.concatenate(
        [
            frame_of[:, None] == frame_range[None, :],
            row_of[:, None] == side_range[None, :],
            column_of[:, None] == side_range[None, :],
        ],
        axis=1,
    ).astype(jnp.float32)
    return (token_valid, memory_valid, select_table, key_onehot)


def pool_field(field, kernel):
    kernel_wide = jnp.tile(kernel, (1, HEADS))
    padded = jnp.pad(field, ((0, 0), (1, 1), (1, 1), (1, 1), (0, 0)))
    accumulated = jnp.zeros_like(field)
    for kernel_tap in range(27):
        frame_shift = kernel_tap // 9
        row_shift = kernel_tap // 3 % 3
        column_shift = kernel_tap % 3
        window = padded[
            :,
            frame_shift : frame_shift + FRAMES,
            row_shift : row_shift + SIDE,
            column_shift : column_shift + SIDE,
            :,
        ]
        accumulated = accumulated + window * kernel_wide[kernel_tap]
    return accumulated


def pool_norm(stacked, pool_weight, pool_gain, pool_bias):
    clip_count = stacked.shape[1]
    results = []
    for branch_index in range(3):
        pooled = pool_field(stacked[branch_index], pool_weight[branch_index])
        per_head = pooled.reshape(clip_count, LENGTH, HEADS, HEAD_DIM)
        results.append(layer_norm(per_head, pool_gain[branch_index], pool_bias[branch_index]))
    return jnp.stack(results)


def build_offsets(queries, rel_table, select_table):
    rel_scores = jnp.einsum("...lhe,re->...lhr", queries, rel_table, precision=HIGHEST)
    return jnp.einsum("...lhr,lpr->...lhp", rel_scores, select_table, precision=HIGHEST)


def extend_last(array_in, width_to):
    extra_cols = width_to - array_in.shape[-1]
    widths = [(0, 0)] * (array_in.ndim - 1) + [(0, extra_cols)]
    return jnp.pad(array_in, widths)


def per_device(
    inputs,
    res_ids,
    memory,
    gain_one,
    bias_one,
    w_qkv,
    b_qkv,
    pool_weight,
    pool_gain,
    pool_bias,
    rel_table,
    w_proj,
    b_proj,
    gain_two,
    bias_two,
    w_up,
    b_up,
    w_down,
    b_down,
    cotangent,
):
    clip_count = res_ids.shape[0]
    row_total = inputs.shape[0]
    scale_factor = HEAD_DIM ** (-0.5)
    ext_width = (HEAD_DIM + OFFSETS + 127) // 128 * 128
    token_valid, memory_valid, select_table, key_onehot = grid_tables(res_ids)
    token_weight = token_valid.reshape(-1).astype(jnp.float32)[:, None]
    wide_inputs = inputs.astype(jnp.float32)
    normed_one, norm_one_back = jax.vjp(layer_norm, wide_inputs, gain_one, bias_one)
    normed_low = normed_one.astype(jnp.bfloat16)
    qkv = jnp.dot(normed_low, w_qkv, preferred_element_type=jnp.float32) + b_qkv
    masked = qkv * token_weight
    stacked = jnp.moveaxis(masked.reshape(clip_count, FRAMES, SIDE, SIDE, 3, D), 4, 0)
    pooled, pool_back = jax.vjp(pool_norm, stacked, pool_weight, pool_gain, pool_bias)
    queries = pooled[0]
    offsets, offset_back = jax.vjp(
        lambda query_in, table_in: build_offsets(query_in, table_in, select_table),
        queries,
        rel_table,
    )
    query_ext = extend_last(
        jnp.concatenate([queries * scale_factor, offsets], axis=-1), ext_width
    ).astype(jnp.bfloat16)
    onehot_heads = jnp.broadcast_to(
        key_onehot[None, :, None, :], (clip_count, LENGTH, HEADS, OFFSETS)
    )
    keys_current = extend_last(
        jnp.concatenate(
            [pooled[1].astype(jnp.bfloat16), onehot_heads.astype(jnp.bfloat16)], axis=-1
        ),
        ext_width,
    )
    memory_heads = memory.reshape(2, clip_count, MEM, HEADS, HEAD_DIM)
    keys_memory = extend_last(memory_heads[0], ext_width)
    keys_ext = jnp.concatenate([keys_current, keys_memory], axis=1)
    values_all = jnp.concatenate([pooled[2].astype(jnp.bfloat16), memory_heads[1]], axis=1)
    valid_all = jnp.concatenate([token_valid, memory_valid], axis=1)[:, None, None, :]

    def masked_scores():
        raw_scores = jnp.einsum(
            "cqhx,ckhx->chqk", query_ext, keys_ext, preferred_element_type=jnp.float32
        )
        return jnp.where(valid_all, raw_scores, -1e30)

    scores = masked_scores()
    row_top = jnp.max(scores, axis=-1, keepdims=True)
    exponents = jnp.exp(scores - row_top)
    row_sum = jnp.sum(exponents, axis=-1, keepdims=True)
    probabilities = exponents / row_sum
    log_total = row_top + jnp.log(row_sum)
    weighted = jnp.einsum(
        "chqk,ckhe->cqhe",
        probabilities.astype(jnp.bfloat16),
        values_all,
        preferred_element_type=jnp.float32,
    )
    attended = (weighted + queries).reshape(row_total, D)
    attended_low = attended.astype(jnp.bfloat16)
    middle = (
        wide_inputs + jnp.dot(attended_low, w_proj, preferred_element_type=jnp.float32) + b_proj
    )
    normed_two, norm_two_back = jax.vjp(layer_norm, middle, gain_two, bias_two)
    rows_low = normed_two.astype(jnp.bfloat16)
    grad_out = cotangent.astype(jnp.float32) * token_weight
    grad_b_down = jnp.sum(grad_out, axis=0)
    grad_out_low = grad_out.astype(jnp.bfloat16)
    gathered = lax.all_gather(rows_low, "tensor", axis=0, tiled=True)
    hidden = jnp.dot(gathered, w_up, preferred_element_type=jnp.float32) + b_up.astype(jnp.float32)
    activated, gelu_back = jax.vjp(gelu_exact, hidden)
    act_low = activated.astype(jnp.bfloat16)
    row_piece = act_low
    mlp_sum = lax.psum_scatter(
        jnp.dot(row_piece, w_down, preferred_element_type=jnp.float32).astype(jnp.bfloat16),
        "tensor",
        scatter_dimension=0,
        tiled=True,
    ).astype(jnp.float32)
    grad_rows = lax.all_gather(grad_out_low, "tensor", axis=0, tiled=True)
    grad_w_down = jnp.einsum("rf,rd->fd", act_low, grad_rows, preferred_element_type=jnp.float32)
    grad_act = jnp.einsum("rd,fd->rf", grad_rows, w_down, preferred_element_type=jnp.float32)
    grad_hidden = gelu_back(grad_act)[0]
    grad_b_up = jnp.sum(grad_hidden, axis=0)
    hidden_low = grad_hidden.astype(jnp.bfloat16)
    grad_w_up = jnp.einsum("rd,rf->df", gathered, hidden_low, preferred_element_type=jnp.float32)
    row_piece = hidden_low
    grad_normed_two = lax.psum_scatter(
        jnp.einsum("rf,df->rd", row_piece, w_up, preferred_element_type=jnp.float32),
        "tensor",
        scatter_dimension=0,
        tiled=True,
    )
    output = ((middle + mlp_sum + b_down) * token_weight).astype(jnp.bfloat16)
    grad_from_two = norm_two_back(grad_normed_two)
    grad_middle = grad_out + grad_from_two[0]
    grad_b_proj = jnp.sum(grad_middle, axis=0)
    proj_low = grad_middle.astype(jnp.bfloat16)
    grad_w_proj = jnp.einsum(
        "rd,re->de", attended_low, proj_low, preferred_element_type=jnp.float32
    )
    grad_attended = jnp.einsum("re,de->rd", proj_low, w_proj, preferred_element_type=jnp.float32)
    grad_attended = grad_attended.reshape(clip_count, LENGTH, HEADS, HEAD_DIM)
    weighted_low = grad_attended.astype(jnp.bfloat16)
    probabilities = jnp.exp(masked_scores() - log_total)
    grad_probs = jnp.einsum(
        "cqhe,ckhe->chqk", weighted_low, values_all, preferred_element_type=jnp.float32
    )
    inner_sum = jnp.sum(probabilities * grad_probs, axis=-1, keepdims=True)
    grad_scores = (probabilities * (grad_probs - inner_sum)).astype(jnp.bfloat16)
    grad_query_ext = jnp.einsum(
        "chqk,ckhx->cqhx", grad_scores, keys_ext, preferred_element_type=jnp.float32
    )
    grad_key_ext = jnp.einsum(
        "chqk,cqhx->ckhx", grad_scores[..., :LENGTH], query_ext, preferred_element_type=jnp.float32
    )
    grad_values = jnp.einsum(
        "chqk,cqhe->ckhe",
        probabilities[..., :LENGTH].astype(jnp.bfloat16),
        weighted_low,
        preferred_element_type=jnp.float32,
    )
    offset_grads = offset_back(grad_query_ext[..., HEAD_DIM : HEAD_DIM + OFFSETS])
    grad_queries = grad_query_ext[..., :HEAD_DIM] * scale_factor + grad_attended + offset_grads[0]
    pool_grads = pool_back(jnp.stack([grad_queries, grad_key_ext[..., :HEAD_DIM], grad_values]))
    grad_qkv = jnp.moveaxis(pool_grads[0], 0, 4).reshape(row_total, 3 * D) * token_weight
    grad_b_qkv = jnp.sum(grad_qkv, axis=0)
    qkv_low = grad_qkv.astype(jnp.bfloat16)
    grad_w_qkv = jnp.einsum("rd,rq->dq", normed_low, qkv_low, preferred_element_type=jnp.float32)
    grad_normed_one = jnp.einsum("rq,dq->rd", qkv_low, w_qkv, preferred_element_type=jnp.float32)
    grad_from_one = norm_one_back(grad_normed_one)
    input_grad = grad_middle + grad_from_one[0]
    summed = lax.psum(
        (
            grad_from_one[1],
            grad_from_one[2],
            grad_w_qkv,
            grad_b_qkv,
            pool_grads[1],
            pool_grads[2],
            pool_grads[3],
            offset_grads[1],
            grad_w_proj,
            grad_b_proj,
            grad_from_two[1],
            grad_from_two[2],
            grad_b_down,
        ),
        ("dp", "tensor"),
    )
    mlp_summed = lax.psum((grad_w_up, grad_b_up, grad_w_down), "dp")
    return (
        output,
        input_grad,
        summed[0],
        summed[1],
        summed[2],
        summed[3],
        summed[4],
        summed[5],
        summed[6],
        summed[7],
        summed[8],
        summed[9],
        summed[10],
        summed[11],
        mlp_summed[0],
        mlp_summed[1],
        mlp_summed[2],
        summed[12],
    )


def solution(mesh):
    return jax.shard_map(
        per_device,
        mesh=mesh,
        in_specs=(
            P(("dp", "tensor"), None),
            P(("dp", "tensor")),
            P(None, ("dp", "tensor"), None),
            P(),
            P(),
            P(),
            P(),
            P(),
            P(),
            P(),
            P(),
            P(),
            P(),
            P(),
            P(),
            P(None, "tensor"),
            P("tensor"),
            P("tensor", None),
            P(),
            P(("dp", "tensor"), None),
        ),
        out_specs=(
            P(("dp", "tensor"), None),
            P(("dp", "tensor"), None),
            P(),
            P(),
            P(),
            P(),
            P(),
            P(),
            P(),
            P(),
            P(),
            P(),
            P(),
            P(),
            P(None, "tensor"),
            P("tensor"),
            P("tensor", None),
            P(),
        ),
        check_vma=False,
    )
```

profile of v0, /device:TPU:0, one launch (start us, length us, event | category | flops | bytes accessed | tf_op | source)
XLA Modules:
  0.0 2125.4 jit_solution(17922374645029894747)
XLA Ops:
  125.5 69.1 %add_reduce_fusion.2 = f32[8,10,10,768]{3,2,1,0:T(8,128)} fusion(f32[768]{0:T(1024)S(1)} %copy-done.108, f32[768]{0:T(1024)S(1)} %copy-done.136, f32[768]{0:T(1024)S(1)} %copy-done.144, f32[768]{0:T(1024)S(1)} %copy-done.147, f32[768]{0:T(1024)S(1)} %copy-done.150, f32[768]{0:T(1024)S(1)} %copy-done.153, f32[768]{0:T(1024)S(1)} %copy-done.155, ...), kind=kLoop, calls=%fused_computation.210 | loop fusion | flops 32563200 | bytes 7455744 | tf_op jit(solution)/shard_map/jvp()/add | solution.py:88
  268.0 76.3 %add_reduce_fusion.1 = f32[8,10,10,768]{3,2,1,0:T(8,128)} fusion(f32[768]{0:T(1024)S(1)} %tile.497, f32[768]{0:T(1024)} %tile.495, f32[768]{0:T(1024)} %tile.493, f32[768]{0:T(1024)} %tile.491, f32[768]{0:T(1024)} %tile.489, f32[768]{0:T(1024)} %tile.487, f32[768]{0:T(1024)} %tile.485, f32[768]{0:T(1024)} %tile.483, f32[768]{0:T(1024)} %tile.481, ...), kind=kLoop, calls=%fused_computation.208 | loop fusion | flops 32563200 | bytes 7455744 | tf_op jit(solution)/shard_map/jvp()/add | solution.py:88
  420.0 76.1 %fusion.116 = (f32[8,10,10,768]{3,2,1,0:T(8,128)}, f32[1,8,10,10,768]{4,0,3,2,1:T(1,128)}) fusion(f32[768]{0:T(1024)} %tile.443, f32[768]{0:T(1024)} %tile.441, f32[768]{0:T(1024)} %tile.439, f32[768]{0:T(1024)} %tile.437, f32[768]{0:T(1024)} %tile.435, f32[768]{0:T(1024)} %tile.433, f32[768]{0:T(1024)} %tile.431, f32[768]{0:T(1024)} %tile.429, ...), kind=kLoop, calls=%fused_computation.511 | loop fusion | flops 32563200 | bytes 9913344 | tf_op jit(solution)/shard_map/jvp()/add | solution.py:88
  655.4 37.4 %all-gather.3.cloned.1.call-done = bf16[3200,768]{1,0:T(8,128)(2,1)} async-done(((bf16[800,768]{1,0:T(8,128)(2,1)}), bf16[3200,768]{1,0:T(8,128)(2,1)}) %all-gather.3.cloned.1.call-update) | async-done | bytes 4915216 | tf_op jit(solution)/shard_map/all_gather | solution.py:200
  704.0 29.5 %all-gather.5.cloned.1.call-done = bf16[3200,768]{1,0:T(8,128)(2,1)} async-done(((bf16[800,768]{1,0:T(8,128)(2,1)}), bf16[3200,768]{1,0:T(8,128)(2,1)}) %all-gather.5.cloned.1.call-update) | async-done | bytes 4915216 | tf_op jit(solution)/shard_map/all_gather | solution.py:211
  841.3 47.1 %reduce-scatter.3.cloned.1.call-done = bf16[800,768]{1,0:T(8,128)(2,1)} async-done(((bf16[3200,768]{1,0:T(8,128)(2,1)}), bf16[800,768]{1,0:T(8,128)(2,1)}) %reduce-scatter.3.cloned.1.call-update) | async-done | bytes 1228816 | tf_op jit(solution)/shard_map/reduce_scatter | solution.py:205
  913.6 24.3 %fusion.2 = (bf16[1,8,800,1000]{3,2,1,0:T(8,128)(2,1)}, f32[8,800]{1,0:T(8,128)S(1)}) fusion(f32[8,800,1000]{2,1,0:T(8,128)} %get-tuple-element.317, f32[8,800]{1,0:T(8,128)S(1)} %copy-done.77, pred[1000]{0:T(1024)(128)(4,1)S(1)} %copy-done.212, f32[8,800,1000]{2,1,0:T(8,128)} %fusion.57), kind=kLoop, calls=%fused_computation.8 | loop fusion | flops 31993600 | bytes 64052200 | tf_op jit(solution)/shard_map/exp | solution.py:236
  993.0 35.6 %multiply_reduce_fusion.62 = (f32[768]{0:T(1024)}, f32[768]{0:T(1024)}, f32[768]{0:T(1024)}, f32[768]{0:T(1024)}, f32[768]{0:T(1024)}, /*index=5*/f32[768]{0:T(1024)}, f32[768]{0:T(1024)}, f32[768]{0:T(1024)}, f32[768]{0:T(1024)}) fusion(f32[1,8,10,10,768]{4,0,3,2,1:T(1,128)} %reshape.3234, f32[1,8,10,10,768]{4,0,3,2,1:T(1,128)} %get-tuple-element.142), kind=kLoop, calls=%fused_computation.166 | loop fusion | flops 11052288 | bytes 4942848 | tf_op jit(solution)/shard_map/transpose(jvp())/reduce_sum | solution.py:88
  1028.7 26.9 %multiply_reduce_fusion.63 = (f32[768]{0:T(1024)}, f32[768]{0:T(1024)}, f32[768]{0:T(1024)}, f32[768]{0:T(1024)}, f32[768]{0:T(1024)}, /*index=5*/f32[768]{0:T(1024)}, f32[768]{0:T(1024)}, f32[768]{0:T(1024)}, f32[768]{0:T(1024)}) fusion(f32[1,8,10,10,768]{4,0,3,2,1:T(1,128)S(1)} %copy-done.2, f32[1,8,10,10,768]{4,0,3,2,1:T(1,128)S(1)} %copy-done.15), kind=kLoop, calls=%fused_computation.167 | loop fusion | flops 11052288 | bytes 4942848 | tf_op jit(solution)/shard_map/transpose(jvp())/reduce_sum | solution.py:88
  1076.0 35.6 %multiply_reduce_fusion.89 = (f32[768]{0:T(1024)}, f32[768]{0:T(1024)}, f32[768]{0:T(1024)}, f32[768]{0:T(1024)}, f32[768]{0:T(1024)}, /*index=5*/f32[768]{0:T(1024)}, f32[768]{0:T(1024)}, f32[768]{0:T(1024)}, f32[768]{0:T(1024)}) fusion(f32[1,8,10,10,768]{4,0,3,2,1:T(1,128)} %reshape.3232, f32[1,8,10,10,768]{4,0,3,2,1:T(1,128)} %copy-done.17), kind=kLoop, calls=%fused_computation.193 | loop fusion | flops 11052288 | bytes 4942848 | tf_op jit(solution)/shard_map/transpose(jvp())/reduce_sum | solution.py:88
  1111.6 26.9 %multiply_reduce_fusion.90 = (f32[768]{0:T(1024)}, f32[768]{0:T(1024)}, f32[768]{0:T(1024)}, f32[768]{0:T(1024)}, f32[768]{0:T(1024)}, /*index=5*/f32[768]{0:T(1024)}, f32[768]{0:T(1024)}, f32[768]{0:T(1024)}, f32[768]{0:T(1024)}) fusion(f32[1,8,10,10,768]{4,0,3,2,1:T(1,128)S(1)} %copy-done.5, f32[1,8,10,10,768]{4,0,3,2,1:T(1,128)S(1)} %copy-done.18), kind=kLoop, calls=%fused_computation.194 | loop fusion | flops 11052288 | bytes 4942848 | tf_op jit(solution)/shard_map/transpose(jvp())/reduce_sum | solution.py:88
  1149.1 26.9 %multiply_reduce_fusion.88 = (f32[768]{0:T(1024)}, f32[768]{0:T(1024)}, f32[768]{0:T(1024)}, f32[768]{0:T(1024)}, f32[768]{0:T(1024)}, /*index=5*/f32[768]{0:T(1...) fusion(f32[1,8,10,10,768]{4,0,3,2,1:T(1,128)} %reshape.3232, ...), kind=kLoop, calls=%fused_computation.192 | loop fusion | flops 11053056 | bytes 9861120 | tf_op jit(solution)/shard_map/transpose(jvp())/reduce_sum | solution.py:88
  1176.1 23.8 %multiply_reduce_fusion.61 = (f32[768]{0:T(1024)}, f32[768]{0:T(1024)}, f32[768]{0:T(1024)}, f32[768]{0:T(1024)}, f32[768]{0:T(1024)}, /*index=5*/f32[768]{0:T(1...) fusion(f32[1,8,10,10,768]{4,0,3,2,1:T(1,128)S(1)} %copy-done.3, ...), kind=kLoop, calls=%fused_computation.165 | loop fusion | flops 11053056 | bytes 9861120 | tf_op jit(solution)/shard_map/transpose(jvp())/reduce_sum | solution.py:88
  1256.4 35.1 %multiply_reduce_fusion.35 = (f32[768]{0:T(1024)S(1)}, f32[768]{0:T(1024)S(1)}, f32[768]{0:T(1024)S(1)}, f32[768]{0:T(1024)S(1)}, f32[768]{0:T(1024)S(1)}, /*ind...) fusion(f32[1,8,10,10,768]{4,0,3,2,1:T(1,128)} %reshape.3237, ...), kind=kLoop, calls=%fused_computation.139 | loop fusion | flops 11052288 | bytes 4942848 | tf_op jit(solution)/shard_map/transpose(jvp())/reduce_sum | solution.py:88
  1291.6 26.3 %multiply_reduce_fusion.36 = (f32[768]{0:T(1024)S(1)}, f32[768]{0:T(1024)S(1)}, f32[768]{0:T(1024)S(1)}, f32[768]{0:T(1024)S(1)}, f32[768]{0:T(1024)S(1)}, /*ind...) fusion(f32[1,8,10,10,768]{4,0,3,2,1:T(1,128)S(1)} %copy-done.11, ...), kind=kLoop, calls=%fused_computation.140 | loop fusion | flops 11052288 | bytes 4942848 | tf_op jit(solution)/shard_map/transpose(jvp())/reduce_sum | solution.py:88
  1362.4 23.0 %multiply_reduce_fusion.77 = (f32[768]{0:T(1024)}, f32[768]{0:T(1024)S(1)}, f32[768]{0:T(1024)S(1)}, f32[1,8,10,10,768]{4,0,3,2,1:T(1,128)S(1)}, f32[1,8,10,10,7...) fusion(f32[1,8,10,10,768]{4,0,3,2,1:T(1,128)S(1)} %copy-done.6,, ...), kind=kLoop, calls=%fused_computation.181 | loop fusion | flops 11671296 | bytes 46743552 | tf_op jit(solution)/shard_map/transpose(jvp())/reduce_sum | solution.py:88
  1406.4 31.8 %broadcast_multiply_fusion = (f32[1,8,10,10,768]{4,0,3,2,1:T(1,128)}, f32[1,8,10,10,768]{4,0,3,2,1:T(1,128)}, f32[1,8,10,10,768]{4,0,3,2,1:T(1,128)}, f32[1,8,10...) fusion(f32[1,8,10,10,768]{4,0,3,2,1:T(1,128)S(1)} %copy-done.4,, ...), kind=kLoop, calls=%fused_computation.224 | loop fusion | flops 11059200 | bytes 46749696 | tf_op jit(solution)/shard_map/transpose(jvp())/mul | solution.py:88
  1438.4 30.9 %broadcast_multiply_fusion.54 = (f32[1,8,10,10,768]{4,0,3,2,1:T(1,128)}, f32[1,8,10,10,768]{4,0,3,2,1:T(1,128)}, f32[1,8,10,10,768]{4,0,3,2,1:T(1,128)}, f32[1,8...) fusion(f32[1,8,10,10,768]{4,0,3,2,1:T(1,128)S(1)} %copy-done.6,, ...), kind=kLoop, calls=%fused_computation.278 | loop fusion | flops 11059200 | bytes 46749696 | tf_op jit(solution)/shard_map/transpose(jvp())/mul | solution.py:88
  1482.6 60.1 %pad_add_fusion.1 = f32[1,10,12,12,768]{4,0,3,2,1:T(1,128)S(1)} fusion(f32[1,8,10,10,768]{4,0,3,2,1:T(1,128)S(1)} %get-tuple-element.155, f32[1,8,10,10,768]{4,0,3,2,1:T(1,128)S(1)} %get-tuple-element.156, f32[1,8,10,10,768]{4,0,3,2,1:T(1,128)S(1)} %get-tuple-element.157, f32[1,8,10,10,768]{4,0,3,2,1:T(1,128)S(1)} %copy-done.37, ...), kind=kLoop, calls=%fused_computation.30 | loop fusion | flops 22118400 | bytes 56033280 | tf_op jit(solution)/shard_map/transpose(jvp())/add_any | solution.py:81
  1549.2 61.8 %pad_add_fusion.2 = f32[1,10,12,12,768]{4,0,3,2,1:T(1,128)S(1)} fusion(f32[1,8,10,10,768]{4,0,3,2,1:T(1,128)} %get-tuple-element.194, f32[1,8,10,10,768]{4,0,3,2,1:T(1,128)} %get-tuple-element.195, f32[1,8,10,10,768]{4,0,3,2,1:T(1,128)} %get-tuple-element.196, f32[1,8,10,10,768]{4,0,3,2,1:T(1,128)} %get-tuple-element.197, ...), kind=kLoop, calls=%fused_computation.31 | loop fusion | flops 22118400 | bytes 56033280 | tf_op jit(solution)/shard_map/transpose(jvp())/add_any | solution.py:81
  1617.5 61.5 %pad_add_fusion.3 = f32[1,10,12,12,768]{4,0,3,2,1:T(1,128)S(1)} fusion(f32[1,8,10,10,768]{4,0,3,2,1:T(1,128)} %get-tuple-element.169, f32[1,8,10,10,768]{4,0,3,2,1:T(1,128)} %get-tuple-element.170, f32[1,8,10,10,768]{4,0,3,2,1:T(1,128)} %get-tuple-element.171, f32[1,8,10,10,768]{4,0,3,2,1:T(1,128)} %get-tuple-element.172, ...), kind=kLoop, calls=%fused_computation.32 | loop fusion | flops 22118400 | bytes 56033280 | tf_op jit(solution)/shard_map/transpose(jvp())/add_any | solution.py:81
  1778.4 22.1 %psum.125 = f32[768]{0:T(1024)} all-reduce(f32[768]{0:T(1024)S(1)} %copy-done.227), channel_id=1, replica_groups=mesh['dp'=8,'tensor'=4] {'dp'}, use_global_device_ids=true, to_apply=%region_135.136 | all-reduce | flops 768 | bytes 6144 | tf_op jit(solution)/shard_map/psum | solution.py:282
  1800.5 100.9 %all-reduce.187.cloned.1.call-done = (f32[768]{0:T(1024)}, f32[768]{0:T(1024)}, f32[2304]{0:T(1024)}, f32[3,27,96]{2,1,0:T(8,128)}, f32[3,96]{1,0:T(4,128)}, /*i...) async-done(((f32[768]{0:T(1024)}, f32[768]{0:T(1024)}, f32[2304]{0:T(1024)}, ...) | async-done | bytes 81424 | tf_op jit(solution)/shard_map/psum | solution.py:264
  1901.4 197.9 %all-reduce.189.cloned.1.call-done = (f32[768,2304]{1,0:T(8,128)}, f32[768,768]{1,0:T(8,128)}) async-done(((f32[768,2304]{1,0:T(8,128)}, f32[768,768]{1,0:T(8,128)}), (f32[768,2304]{1,0:T(8,128)}, f32[768,768]{1,0:T(8,128)})) %all-reduce.189.cloned.1.call-update) | async-done | bytes 9437200 | tf_op jit(solution)/shard_map/psum | solution.py:264
  (948 shorter events, 919.5 us)
Async XLA Ops:
  7.2 81.0 %copy-start = (bf16[768,2304]{1,0:T(8,128)(2,1)S(1)}, bf16[768,2304]{1,0:T(8,128)(2,1)}, u32[]{:S(2)}) copy-start(bf16[768,2304]{1,0:T(8,128)(2,1)} %param.25) | copy-start | bytes 10616836
  7.2 685.6 %all-gather.3.cloned.1.call-start = ((), (), s32[]{:S(2)}) async-start(), calls=%async_computation.2 | async-start | bytes 6144000 | tf_op jit(solution)/shard_map/all_gather | solution.py:200
  9.3 884.1 %copy-start.87 = (f32[800]{0:T(1024)}, f32[800]{0:T(1024)S(1)}, u32[]{:S(2)}) copy-start(f32[800]{0:T(1024)S(1)} %or_convert_fusion.1) | copy-start | bytes 9604
  21.0 102.9 %copy-start.100 = (f32[768]{0:T(1024)}, f32[768]{0:T(1024)S(1)}, u32[]{:S(2)}) copy-start(f32[768]{0:T(1024)S(1)} %tile.345) | copy-start | bytes 9220
  24.6 71.2 %copy-start.89 = (f32[800]{0:T(1024)}, f32[800]{0:T(1024)S(1)}, u32[]{:S(2)}) copy-start(f32[800]{0:T(1024)S(1)} %broadcast_multiply_fusion.85) | copy-start | bytes 9604
  27.0 68.8 %copy-start.98 = (f32[800]{0:T(1024)}, f32[800]{0:T(1024)S(1)}, u32[]{:S(2)}) copy-start(f32[800]{0:T(1024)S(1)} %fusion.91) | copy-start | bytes 9604
  205.3 139.0 %copy-start.138 = (f32[768]{0:T(1024)}, f32[768]{0:T(1024)S(1)}, u32[]{:S(2)}) copy-start(f32[768]{0:T(1024)S(1)} %tile.497) | copy-start | bytes 9220
  206.7 137.6 %copy-start.140 = (f32[768]{0:T(1024)}, f32[768]{0:T(1024)S(1)}, u32[]{:S(2)}) copy-start(f32[768]{0:T(1024)S(1)} %tile.457) | copy-start | bytes 9220
  208.7 135.5 %copy-start.142 = (f32[768]{0:T(1024)}, f32[768]{0:T(1024)S(1)}, u32[]{:S(2)}) copy-start(f32[768]{0:T(1024)S(1)} %tile.455) | copy-start | bytes 9220
  355.1 141.0 %copy-start.181 = (f32[768]{0:T(1024)}, f32[768]{0:T(1024)S(1)}, u32[]{:S(2)}) copy-start(f32[768]{0:T(1024)S(1)} %tile.421) | copy-start | bytes 9220
  355.8 140.3 %copy-start.183 = (f32[768]{0:T(1024)}, f32[768]{0:T(1024)S(1)}, u32[]{:S(2)}) copy-start(f32[768]{0:T(1024)S(1)} %tile.419) | copy-start | bytes 9220
  357.8 138.3 %copy-start.185 = (f32[768]{0:T(1024)}, f32[768]{0:T(1024)S(1)}, u32[]{:S(2)}) copy-start(f32[768]{0:T(1024)S(1)} %tile.417) | copy-start | bytes 9220
  508.1 120.5 %copy-start.208 = (f32[96]{0:T(128)}, f32[96]{0:T(128)S(1)}, u32[]{:S(2)}) copy-start(f32[96]{0:T(128)S(1)} %get-tuple-element.312) | copy-start | bytes 1156
  651.4 82.2 %all-gather.5.cloned.1.call-start = ((), (), s32[]{:S(2)}) async-start(), calls=%async_computation.4 | async-start | bytes 6144000 | tf_op jit(solution)/shard_map/all_gather | solution.py:211
  654.0 182.7 %reduce-scatter.5.cloned.1.call-start = ((), (), s32[]{:S(2)}) async-start(), calls=%async_computation.5 | async-start | bytes 12288000 | tf_op jit(solution)/shard_map/reduce_scatter | solution.py:219
  755.6 132.8 %reduce-scatter.3.cloned.1.call-start = ((), (), s32[]{:S(2)}) async-start(), calls=%async_computation.3 | async-start | bytes 6144000 | tf_op jit(solution)/shard_map/reduce_scatter | solution.py:205
  765.6 1034.9 %all-reduce.191.cloned.1.call-start = ((), (), s32[]{:S(2)}) async-start(), calls=%async_computation.8 | async-start | bytes 9437184 | tf_op jit(solution)/shard_map/psum | solution.py:282
  830.1 1071.3 %all-reduce.187.cloned.1.call-start = ((), (), s32[]{:S(2)}) async-start(), calls=%async_computation.6 | async-start | bytes 237568 | tf_op jit(solution)/shard_map/psum | solution.py:264
  1549.1 136.4 %copy-start.24 = (f32[1,1,8,10,10,768]{5,0,4,3,2,1:T(1,128)}, f32[1,1,8,10,10,768]{5,0,4,3,2,1:T(1,128)S(1)}, u32[]{:S(2)}) copy-start(f32[1,1,8,10,10,768]{5,0,4,3,2,1:T(1,128)S(1)} %fusion.37) | copy-start | bytes 7372804
  1549.1 61.9 %copy-start.35 = (f32[1,8,10,10,768]{4,0,3,2,1:T(1,128)S(1)}, f32[1,8,10,10,768]{4,0,3,2,1:T(1,128)}, u32[]{:S(2)}) copy-start(f32[1,8,10,10,768]{4,0,3,2,1:T(1,128)} %get-tuple-element.147) | copy-start | bytes 7372804
  1549.1 61.9 %copy-start.36 = (f32[1,8,10,10,768]{4,0,3,2,1:T(1,128)S(1)}, f32[1,8,10,10,768]{4,0,3,2,1:T(1,128)}, u32[]{:S(2)}) copy-start(f32[1,8,10,10,768]{4,0,3,2,1:T(1,128)} %get-tuple-element.148) | copy-start | bytes 7372804
  1549.1 61.9 %copy-start.38 = (f32[1,8,10,10,768]{4,0,3,2,1:T(1,128)S(1)}, f32[1,8,10,10,768]{4,0,3,2,1:T(1,128)}, u32[]{:S(2)}) copy-start(f32[1,8,10,10,768]{4,0,3,2,1:T(1,128)} %get-tuple-element.190) | copy-start | bytes 7372804
  1617.4 68.0 %copy-start.25 = (f32[1,1,8,10,10,768]{5,0,4,3,2,1:T(1,128)}, f32[1,1,8,10,10,768]{5,0,4,3,2,1:T(1,128)S(1)}, u32[]{:S(2)}) copy-start(f32[1,1,8,10,10,768]{5,0,4,3,2,1:T(1,128)S(1)} %fusion.38) | copy-start | bytes 7372804
  1772.2 327.1 %all-reduce.189.cloned.1.call-start = ((), (), s32[]{:S(2)}) async-start(), calls=%async_computation.7 | async-start | bytes 18874368 | tf_op jit(solution)/shard_map/psum | solution.py:264
  (237 other events, 3869.5 us)
Sparse Core Ops, SparseCore 0:
  651.5 41.2 all-gather.2
  694.9 38.5 all-gather.4
  755.7 80.9 reduce-scatter.4
  839.2 49.1 reduce-scatter.2
  892.9 169.9 all-reduce.190
  1772.3 129.0 all-reduce.186
  1908.5 190.7 all-reduce.188
where the time goes:
time: 2140 us; the launch traced here: 2130 us
  other arithmetic  1000 us (47%)
  local copies, waits for them, and re-layouts  457 us (21%)
  waiting for transfers between devices  420 us (20%)
  matrix products  205 us (10%)
  blocking collectives  22.1 us (1%)
    psum x2, waiting for transfers between devices, per_device(): lax.psum((grad_from_one[1], grad_from_one[2], grad_w_qkv, grad_b_qkv, poo...  299 us
    reduce_sum x10, other arithmetic, pool_field(): accumulated = accumulated + window * kernel_wide[kernel_tap]  282 us
    add x3, other arithmetic, pool_field(): accumulated = accumulated + window * kernel_wide[kernel_tap]  221 us
    another operation x162, local copies, waits for them, and re-layouts, pool_field(): kernel_wide = jnp.tile(kernel, (1, HEADS))  191 us
    add_any x3, other arithmetic, pool_field(): padded[:, frame_shift:frame_shift + FRAMES, row_shift:row_shift + SIDE, c...  183 us
    mul x5, other arithmetic, pool_field(): accumulated = accumulated + window * kernel_wide[kernel_tap]  105 us
    reshape x10, local copies, waits for them, and re-layouts, pool_norm(): per_head = pooled.reshape(clip_count, LENGTH, HEADS, HEAD_DIM)  54.4 us
    reduce_scatter x1, waiting for transfers between devices, per_device(): lax.psum_scatter(jnp.dot(row_piece, w_down, preferred_element_type=jnp.fl...  47.1 us
  transfers between devices with their start and end apart: 7, of which 6 were waited for; matrix products, arithmetic and copies ran while one was open for 46% of the time, Pallas kernels for 0%

commit v1 on v0

--- a/solution.py
+++ b/solution.py
@@ -1,3 +1,4 @@
+import functools
 import jax
 import jax.numpy as jnp
 from jax import lax
@@ -16,6 +17,13 @@
 HIGHEST = lax.Precision.HIGHEST
 NORM_EPS = 1e-06
 INV_ROOT_TWO = 0.7071067811865476
+
+
+def manage_rates_up(z, lane_axis, axis_key):
+    return lax.psum(lax.psum(z, axis_key), lane_axis)
+
+
+feed_the_pools = functools.partial(manage_rates_up, lane_axis="dp", axis_key="tensor")
 
 
 def layer_norm(values, gain_vec, shift_vec):
@@ -261,7 +269,7 @@
     grad_normed_one = jnp.einsum("rq,dq->rd", qkv_low, w_qkv, preferred_element_type=jnp.float32)
     grad_from_one = norm_one_back(grad_normed_one)
     input_grad = grad_middle + grad_from_one[0]
-    summed = lax.psum(
+    summed = feed_the_pools(
         (
             grad_from_one[1],
             grad_from_one[2],
@@ -276,8 +284,7 @@
             grad_from_two[1],
             grad_from_two[2],
             grad_b_down,
-        ),
-        ("dp", "tensor"),
+        )
     )
     mlp_summed = lax.psum((grad_w_up, grad_b_up, grad_w_down), "dp")
     return (

time: 2140 us -> 2550 us (1.19)
  waiting for transfers between devices: 420 us -> 846 us
    psum x3 -> x4, waiting for transfers between devices: 299 us -> 706 us  [manage_rates_up(): return lax.psum(lax.psum(z, axis_key), lane_axis)]
  transfers between devices with their start and end apart: 7 -> 8, of which waited for: 6 -> 8; matrix products, arithmetic and copies ran while one was open for 46% -> 4% of each run, Pallas kernels for 0% -> 0%
where the time goes in v1:
time: 2550 us; the launch traced here: 2540 us
  other arithmetic  1010 us (40%)
  waiting for transfers between devices  846 us (33%)
  local copies, waits for them, and re-layouts  454 us (18%)
  matrix products  210 us (8%)
    psum x4, waiting for transfers between devices, manage_rates_up(): return lax.psum(lax.psum(z, axis_key), lane_axis)  706 us
    reduce_sum x10, other arithmetic, pool_field(): accumulated = accumulated + window * kernel_wide[kernel_tap]  283 us
    add x3, other arithmetic, pool_field(): accumulated = accumulated + window * kernel_wide[kernel_tap]  222 us
    another operation x162, local copies, waits for them, and re-layouts, pool_field(): kernel_wide = jnp.tile(kernel, (1, HEADS))  190 us
    add_any x3, other arithmetic, pool_field(): padded[:, frame_shift:frame_shift + FRAMES, row_shift:row_shift + SIDE, c...  184 us
    mul x5, other arithmetic, pool_field(): accumulated = accumulated + window * kernel_wide[kernel_tap]  105 us
    reshape x10, local copies, waits for them, and re-layouts, pool_norm(): per_head = pooled.reshape(clip_count, LENGTH, HEADS, HEAD_DIM)  54.4 us
  transfers between devices with their start and end apart: 8, of which 8 were waited for; matrix products, arithmetic and copies ran while one was open for 4% of the time, Pallas kernels for 0%

profile of v1, /device:TPU:0, one launch (start us, length us, event | category | flops | bytes accessed | tf_op | source)
XLA Modules:
  0.0 2543.2 jit_solution(4869420801762791247)
XLA Ops:
  125.2 69.1 %add_reduce_fusion.2 = f32[8,10,10,768]{3,2,1,0:T(8,128)} fusion(f32[768]{0:T(1024)S(1)} %copy-done.109, f32[768]{0:T(1024)S(1)} %copy-done.137, f32[768]{0:T(1024)S(1)} %copy-done.145, f32[768]{0:T(1024)S(1)} %copy-done.148, f32[768]{0:T(1024)S(1)} %copy-done.151, f32[768]{0:T(1024)S(1)} %copy-done.154, f32[768]{0:T(1024)S(1)} %copy-done.156, ...), kind=kLoop, calls=%fused_computation.210 | loop fusion | flops 32563200 | bytes 7455744 | tf_op jit(solution)/shard_map/jvp()/add | solution.py:96
  267.7 76.4 %add_reduce_fusion.1 = f32[8,10,10,768]{3,2,1,0:T(8,128)} fusion(f32[768]{0:T(1024)S(1)} %tile.497, f32[768]{0:T(1024)} %tile.495, f32[768]{0:T(1024)} %tile.493, f32[768]{0:T(1024)} %tile.491, f32[768]{0:T(1024)} %tile.489, f32[768]{0:T(1024)} %tile.487, f32[768]{0:T(1024)} %tile.485, f32[768]{0:T(1024)} %tile.483, f32[768]{0:T(1024)} %tile.481, ...), kind=kLoop, calls=%fused_computation.208 | loop fusion | flops 32563200 | bytes 7455744 | tf_op jit(solution)/shard_map/jvp()/add | solution.py:96
  419.3 76.2 %fusion.116 = (f32[8,10,10,768]{3,2,1,0:T(8,128)}, f32[1,8,10,10,768]{4,0,3,2,1:T(1,128)}) fusion(f32[768]{0:T(1024)} %tile.443, f32[768]{0:T(1024)} %tile.441, f32[768]{0:T(1024)} %tile.439, f32[768]{0:T(1024)} %tile.437, f32[768]{0:T(1024)} %tile.435, f32[768]{0:T(1024)} %tile.433, f32[768]{0:T(1024)} %tile.431, f32[768]{0:T(1024)} %tile.429, ...), kind=kLoop, calls=%fused_computation.511 | loop fusion | flops 32563200 | bytes 9913344 | tf_op jit(solution)/shard_map/jvp()/add | solution.py:96
  654.7 37.4 %all-gather.3.cloned.1.call-done = bf16[3200,768]{1,0:T(8,128)(2,1)} async-done(((bf16[800,768]{1,0:T(8,128)(2,1)}), bf16[3200,768]{1,0:T(8,128)(2,1)}) %all-gather.3.cloned.1.call-update) | async-done | bytes 4915216 | tf_op jit(solution)/shard_map/all_gather | solution.py:208
  703.4 29.5 %all-gather.5.cloned.1.call-done = bf16[3200,768]{1,0:T(8,128)(2,1)} async-done(((bf16[800,768]{1,0:T(8,128)(2,1)}), bf16[3200,768]{1,0:T(8,128)(2,1)}) %all-gather.5.cloned.1.call-update) | async-done | bytes 4915216 | tf_op jit(solution)/shard_map/all_gather | solution.py:219
  810.5 25.5 %reduce-scatter.5.cloned.1.call-done = f32[800,768]{1,0:T(8,128)} async-done(((f32[3200,768]{1,0:T(8,128)}), f32[800,768]{1,0:T(8,128)}) %reduce-scatter.5.cloned.1.call-update) | async-done | bytes 2457616 | tf_op jit(solution)/shard_map/reduce_scatter | solution.py:227
  840.7 47.7 %reduce-scatter.3.cloned.1.call-done = bf16[800,768]{1,0:T(8,128)(2,1)} async-done(((bf16[3200,768]{1,0:T(8,128)(2,1)}), bf16[800,768]{1,0:T(8,128)(2,1)}) %reduce-scatter.3.cloned.1.call-update) | async-done | bytes 1228816 | tf_op jit(solution)/shard_map/reduce_scatter | solution.py:213
  913.2 24.4 fusion.2
  992.0 35.9 %multiply_reduce_fusion.62 = (f32[768]{0:T(1024)}, f32[768]{0:T(1024)}, f32[768]{0:T(1024)}, f32[768]{0:T(1024)}, f32[768]{0:T(1024)}, /*index=5*/f32[768]{0:T(1024)}, f32[768]{0:T(1024)}, f32[768]{0:T(1024)}, f32[768]{0:T(1024)}) fusion(f32[1,8,10,10,768]{4,0,3,2,1:T(1,128)} %reshape.3234, f32[1,8,10,10,768]{4,0,3,2,1:T(1,128)} %get-tuple-element.156), kind=kLoop, calls=%fused_computation.166 | loop fusion | flops 11052288 | bytes 4942848 | tf_op jit(solution)/shard_map/transpose(jvp())/reduce_sum | solution.py:96
  1028.0 26.9 %multiply_reduce_fusion.63 = (f32[768]{0:T(1024)}, f32[768]{0:T(1024)}, f32[768]{0:T(1024)}, f32[768]{0:T(1024)}, f32[768]{0:T(1024)}, /*index=5*/f32[768]{0:T(1024)}, f32[768]{0:T(1024)}, f32[768]{0:T(1024)}, f32[768]{0:T(1024)}) fusion(f32[1,8,10,10,768]{4,0,3,2,1:T(1,128)S(1)} %copy-done.2, f32[1,8,10,10,768]{4,0,3,2,1:T(1,128)S(1)} %copy-done.16), kind=kLoop, calls=%fused_computation.167 | loop fusion | flops 11052288 | bytes 4942848 | tf_op jit(solution)/shard_map/transpose(jvp())/reduce_sum | solution.py:96
  1083.0 35.7 %multiply_reduce_fusion.89 = (f32[768]{0:T(1024)}, f32[768]{0:T(1024)}, f32[768]{0:T(1024)}, f32[768]{0:T(1024)}, f32[768]{0:T(1024)}, /*index=5*/f32[768]{0:T(1024)}, f32[768]{0:T(1024)}, f32[768]{0:T(1024)}, f32[768]{0:T(1024)}) fusion(f32[1,8,10,10,768]{4,0,3,2,1:T(1,128)} %reshape.3232, f32[1,8,10,10,768]{4,0,3,2,1:T(1,128)} %copy-done.18), kind=kLoop, calls=%fused_computation.193 | loop fusion | flops 11052288 | bytes 4942848 | tf_op jit(solution)/shard_map/transpose(jvp())/reduce_sum | solution.py:96
  1118.7 27.1 %multiply_reduce_fusion.90 = (f32[768]{0:T(1024)}, f32[768]{0:T(1024)}, f32[768]{0:T(1024)}, f32[768]{0:T(1024)}, f32[768]{0:T(1024)}, /*index=5*/f32[768]{0:T(1024)}, f32[768]{0:T(1024)}, f32[768]{0:T(1024)}, f32[768]{0:T(1024)}) fusion(f32[1,8,10,10,768]{4,0,3,2,1:T(1,128)S(1)} %copy-done.5, f32[1,8,10,10,768]{4,0,3,2,1:T(1,128)S(1)} %copy-done.19), kind=kLoop, calls=%fused_computation.194 | loop fusion | flops 11052288 | bytes 4942848 | tf_op jit(solution)/shard_map/transpose(jvp())/reduce_sum | solution.py:96
  1156.4 26.9 %multiply_reduce_fusion.88 = (f32[768]{0:T(1024)}, f32[768]{0:T(1024)}, f32[768]{0:T(1024)}, f32[768]{0:T(1024)}, f32[768]{0:T(1024)}, /*index=5*/f32[768]{0:T(1...) fusion(f32[1,8,10,10,768]{4,0,3,2,1:T(1,128)} %reshape.3232, ...), kind=kLoop, calls=%fused_computation.192 | loop fusion | flops 11053056 | bytes 9861120 | tf_op jit(solution)/shard_map/transpose(jvp())/reduce_sum | solution.py:96
  1183.4 23.8 multiply_reduce_fusion.61
  1263.7 35.8 %multiply_reduce_fusion.35 = (f32[768]{0:T(1024)}, f32[768]{0:T(1024)}, f32[768]{0:T(1024)}, f32[768]{0:T(1024)}, f32[768]{0:T(1024)}, /*index=5*/f32[768]{0:T(1024)}, f32[768]{0:T(1024)}, f32[768]{0:T(1024)}, f32[768]{0:T(1024)}) fusion(f32[1,8,10,10,768]{4,0,3,2,1:T(1,128)} %reshape.3237, f32[1,8,10,10,768]{4,0,3,2,1:T(1,128)} %get-tuple-element.157), kind=kLoop, calls=%fused_computation.139 | loop fusion | flops 11052288 | bytes 4942848 | tf_op jit(solution)/shard_map/transpose(jvp())/reduce_sum | solution.py:96
  1299.5 26.9 %multiply_reduce_fusion.36 = (f32[768]{0:T(1024)}, f32[768]{0:T(1024)}, f32[768]{0:T(1024)}, f32[768]{0:T(1024)}, f32[768]{0:T(1024)}, /*index=5*/f32[768]{0:T(1024)}, f32[768]{0:T(1024)}, f32[768]{0:T(1024)}, f32[768]{0:T(1024)}) fusion(f32[1,8,10,10,768]{4,0,3,2,1:T(1,128)S(1)} %copy-done.11, f32[1,8,10,10,768]{4,0,3,2,1:T(1,128)S(1)} %copy-done.15), kind=kLoop, calls=%fused_computation.140 | loop fusion | flops 11052288 | bytes 4942848 | tf_op jit(solution)/shard_map/transpose(jvp())/reduce_sum | solution.py:96
  1414.3 31.8 %broadcast_multiply_fusion = (f32[1,8,10,10,768]{4,0,3,2,1:T(1,128)}, f32[1,8,10,10,768]{4,0,3,2,1:T(1,128)}, f32[1,8,10,10,768]{4,0,3,2,1:T(1,128)}, f32[1,8,10...) fusion(f32[1,8,10,10,768]{4,0,3,2,1:T(1,128)S(1)} %copy-done.4,, ...), kind=kLoop, calls=%fused_computation.224 | loop fusion | flops 11059200 | bytes 46749696 | tf_op jit(solution)/shard_map/transpose(jvp())/mul | solution.py:96
  1446.2 31.0 %broadcast_multiply_fusion.54 = (f32[1,8,10,10,768]{4,0,3,2,1:T(1,128)}, f32[1,8,10,10,768]{4,0,3,2,1:T(1,128)}, f32[1,8,10,10,768]{4,0,3,2,1:T(1,128)}, f32[1,8...) fusion(f32[1,8,10,10,768]{4,0,3,2,1:T(1,128)S(1)} %copy-done.6,, ...), kind=kLoop, calls=%fused_computation.278 | loop fusion | flops 11059200 | bytes 46749696 | tf_op jit(solution)/shard_map/transpose(jvp())/mul | solution.py:96
  1477.2 60.1 %pad_add_fusion.1 = f32[1,10,12,12,768]{4,0,3,2,1:T(1,128)S(1)} fusion(f32[1,8,10,10,768]{4,0,3,2,1:T(1,128)S(1)} %get-tuple-element.169, f32[1,8,10,10,768]{4,0,3,2,1:T(1,128)S(1)} %get-tuple-element.170, f32[1,8,10,10,768]{4,0,3,2,1:T(1,128)S(1)} %get-tuple-element.171, f32[1,8,10,10,768]{4,0,3,2,1:T(1,128)S(1)} %copy-done.38, ...), kind=kLoop, calls=%fused_computation.30 | loop fusion | flops 22118400 | bytes 56033280 | tf_op jit(solution)/shard_map/transpose(jvp())/add_any | solution.py:89
  1543.8 62.1 %pad_add_fusion.2 = f32[1,10,12,12,768]{4,0,3,2,1:T(1,128)S(1)} fusion(f32[1,8,10,10,768]{4,0,3,2,1:T(1,128)} %get-tuple-element.208, f32[1,8,10,10,768]{4,0,3,2,1:T(1,128)} %get-tuple-element.209, f32[1,8,10,10,768]{4,0,3,2,1:T(1,128)} %get-tuple-element.210, f32[1,8,10,10,768]{4,0,3,2,1:T(1,128)} %get-tuple-element.211, ...), kind=kLoop, calls=%fused_computation.31 | loop fusion | flops 22118400 | bytes 56033280 | tf_op jit(solution)/shard_map/transpose(jvp())/add_any | solution.py:89
  1612.4 61.8 %pad_add_fusion.3 = f32[1,10,12,12,768]{4,0,3,2,1:T(1,128)S(1)} fusion(f32[1,8,10,10,768]{4,0,3,2,1:T(1,128)} %get-tuple-element.183, f32[1,8,10,10,768]{4,0,3,2,1:T(1,128)} %get-tuple-element.184, f32[1,8,10,10,768]{4,0,3,2,1:T(1,128)} %get-tuple-element.185, f32[1,8,10,10,768]{4,0,3,2,1:T(1,128)} %get-tuple-element.186, ...), kind=kLoop, calls=%fused_computation.32 | loop fusion | flops 22118400 | bytes 56033280 | tf_op jit(solution)/shard_map/transpose(jvp())/add_any | solution.py:89
  1827.2 165.0 %all-reduce.195.cloned.1.call-done = (f32[768,2304]{1,0:T(8,128)}, f32[768,768]{1,0:T(8,128)}) async-done(((f32[768,2304]{1,0:T(8,128)}, f32[768,768]{1,0:T(8,128)}), (f32[768,2304]{1,0:T(8,128)}, f32[768,768]{1,0:T(8,128)})) %all-reduce.195.cloned.1.call-update) | async-done | bytes 9437200 | tf_op jit(solution)/shard_map/psum | solution.py:23
  1992.2 78.1 %all-reduce.189.cloned.1.call-done = (f32[768]{0:T(1024)}, f32[768]{0:T(1024)}, f32[2304]{0:T(1024)}, f32[3,27,96]{2,1,0:T(8,128)}, f32[3,96]{1,0:T(4,128)}, /*i...) async-done(((f32[768]{0:T(1024)}, f32[768]{0:T(1024)}, f32[2304]{0:T(1024)}, ...) | async-done | bytes 84496 | tf_op jit(solution)/shard_map/psum | solution.py:23
  2070.3 446.4 %all-reduce.191.cloned.1.call-done = (f32[768,2304]{1,0:T(8,128)}, f32[768,768]{1,0:T(8,128)}, f32[768,768]{1,0:T(8,128)}, f32[768,768]{1,0:T(8,128)}) async-done(((f32[768,2304]{1,0:T(8,128)}, f32[768,768]{1,0:T(8,128)}, f32[768,768]{1,0:T(8,128)}, f32[768,768]{1,0:T(8,128)}), (f32[768,2304]{1,0:T(8,128)}, f32[768,768]{1,0:T(8,128)}, f32[768,768]{1,0:T(8,128)}, ...) | async-done | bytes 14155792 | tf_op jit(solution)/shard_map/psum | solution.py:23
  (1043 shorter events, 962.8 us)
Async XLA Ops:
  7.2 80.9 %copy-start = (bf16[768,2304]{1,0:T(8,128)(2,1)S(1)}, bf16[768,2304]{1,0:T(8,128)(2,1)}, u32[]{:S(2)}) copy-start(bf16[768,2304]{1,0:T(8,128)(2,1)} %param.25) | copy-start | bytes 10616836
  7.2 684.9 %all-gather.3.cloned.1.call-start = ((), (), s32[]{:S(2)}) async-start(), calls=%async_computation.2 | async-start | bytes 6144000 | tf_op jit(solution)/shard_map/all_gather | solution.py:208
  9.3 884.1 %copy-start.88 = (f32[800]{0:T(1024)}, f32[800]{0:T(1024)S(1)}, u32[]{:S(2)}) copy-start(f32[800]{0:T(1024)S(1)} %or_convert_fusion.1) | copy-start | bytes 9604
  21.0 102.5 %copy-start.101 = (f32[768]{0:T(1024)}, f32[768]{0:T(1024)S(1)}, u32[]{:S(2)}) copy-start(f32[768]{0:T(1024)S(1)} %tile.345) | copy-start | bytes 9220
  24.6 71.0 %copy-start.90 = (f32[800]{0:T(1024)}, f32[800]{0:T(1024)S(1)}, u32[]{:S(2)}) copy-start(f32[800]{0:T(1024)S(1)} %broadcast_multiply_fusion.85) | copy-start | bytes 9604
  27.0 68.6 %copy-start.99 = (f32[800]{0:T(1024)}, f32[800]{0:T(1024)S(1)}, u32[]{:S(2)}) copy-start(f32[800]{0:T(1024)S(1)} %fusion.91) | copy-start | bytes 9604
  205.0 139.1 %copy-start.139 = (f32[768]{0:T(1024)}, f32[768]{0:T(1024)S(1)}, u32[]{:S(2)}) copy-start(f32[768]{0:T(1024)S(1)} %tile.497) | copy-start | bytes 9220
  206.4 137.7 %copy-start.141 = (f32[768]{0:T(1024)}, f32[768]{0:T(1024)S(1)}, u32[]{:S(2)}) copy-start(f32[768]{0:T(1024)S(1)} %tile.457) | copy-start | bytes 9220
  208.4 135.7 %copy-start.143 = (f32[768]{0:T(1024)}, f32[768]{0:T(1024)S(1)}, u32[]{:S(2)}) copy-start(f32[768]{0:T(1024)S(1)} %tile.455) | copy-start | bytes 9220
  354.9 140.5 %copy-start.182 = (f32[768]{0:T(1024)}, f32[768]{0:T(1024)S(1)}, u32[]{:S(2)}) copy-start(f32[768]{0:T(1024)S(1)} %tile.421) | copy-start | bytes 9220
  355.7 139.8 %copy-start.184 = (f32[768]{0:T(1024)}, f32[768]{0:T(1024)S(1)}, u32[]{:S(2)}) copy-start(f32[768]{0:T(1024)S(1)} %tile.419) | copy-start | bytes 9220
  357.7 137.8 %copy-start.186 = (f32[768]{0:T(1024)}, f32[768]{0:T(1024)S(1)}, u32[]{:S(2)}) copy-start(f32[768]{0:T(1024)S(1)} %tile.417) | copy-start | bytes 9220
  507.5 120.4 %copy-start.208 = (f32[96]{0:T(128)}, f32[96]{0:T(128)S(1)}, u32[]{:S(2)}) copy-start(f32[96]{0:T(128)S(1)} %get-tuple-element.326) | copy-start | bytes 1156
  650.7 82.2 %all-gather.5.cloned.1.call-start = ((), (), s32[]{:S(2)}) async-start(), calls=%async_computation.4 | async-start | bytes 6144000 | tf_op jit(solution)/shard_map/all_gather | solution.py:219
  653.4 182.7 %reduce-scatter.5.cloned.1.call-start = ((), (), s32[]{:S(2)}) async-start(), calls=%async_computation.5 | async-start | bytes 12288000 | tf_op jit(solution)/shard_map/reduce_scatter | solution.py:227
  754.9 133.4 %reduce-scatter.3.cloned.1.call-start = ((), (), s32[]{:S(2)}) async-start(), calls=%async_computation.3 | async-start | bytes 6144000 | tf_op jit(solution)/shard_map/reduce_scatter | solution.py:213
  765.3 1052.4 %all-reduce.193.cloned.1.call-start = ((), (), s32[]{:S(2)}) async-start(), calls=%async_computation.8 | async-start | bytes 237568 | tf_op jit(solution)/shard_map/psum | solution.py:23
  1543.7 137.0 %copy-start.25 = (f32[1,1,8,10,10,768]{5,0,4,3,2,1:T(1,128)}, f32[1,1,8,10,10,768]{5,0,4,3,2,1:T(1,128)S(1)}, u32[]{:S(2)}) copy-start(f32[1,1,8,10,10,768]{5,0,4,3,2,1:T(1,128)S(1)} %fusion.37) | copy-start | bytes 7372804
  1543.7 62.1 %copy-start.36 = (f32[1,8,10,10,768]{4,0,3,2,1:T(1,128)S(1)}, f32[1,8,10,10,768]{4,0,3,2,1:T(1,128)}, u32[]{:S(2)}) copy-start(f32[1,8,10,10,768]{4,0,3,2,1:T(1,128)} %get-tuple-element.161) | copy-start | bytes 7372804
  1543.7 62.1 %copy-start.37 = (f32[1,8,10,10,768]{4,0,3,2,1:T(1,128)S(1)}, f32[1,8,10,10,768]{4,0,3,2,1:T(1,128)}, u32[]{:S(2)}) copy-start(f32[1,8,10,10,768]{4,0,3,2,1:T(1,128)} %get-tuple-element.162) | copy-start | bytes 7372804
  1612.3 68.3 %copy-start.26 = (f32[1,1,8,10,10,768]{5,0,4,3,2,1:T(1,128)}, f32[1,1,8,10,10,768]{5,0,4,3,2,1:T(1,128)S(1)}, u32[]{:S(2)}) copy-start(f32[1,1,8,10,10,768]{5,0,4,3,2,1:T(1,128)S(1)} %fusion.38) | copy-start | bytes 7372804
  1785.8 206.5 %all-reduce.195.cloned.1.call-start = ((), (), s32[]{:S(2)}) async-start(), calls=%async_computation.9 | async-start | bytes 18874368 | tf_op jit(solution)/shard_map/psum | solution.py:23
  1791.3 279.1 %all-reduce.189.cloned.1.call-start = ((), (), s32[]{:S(2)}) async-start(), calls=%async_computation.6 | async-start | bytes 245760 | tf_op jit(solution)/shard_map/psum | solution.py:23
  1817.7 699.0 %all-reduce.191.cloned.1.call-start = ((), (), s32[]{:S(2)}) async-start(), calls=%async_computation.7 | async-start | bytes 28311552 | tf_op jit(solution)/shard_map/psum | solution.py:23
  (284 other events, 5005.0 us)
Sparse Core Ops, SparseCore 0:
  650.8 41.2 all-gather.2
  694.3 38.5 all-gather.4
  755.1 80.9 reduce-scatter.4
  839.1 49.1 reduce-scatter.2
  1785.9 31.7 all-reduce.192
  1821.3 170.9 all-reduce.194
  1997.6 72.6 all-reduce.188
  2076.3 440.3 all-reduce.190
